TPU v7x, 512 devices: a whole 4x8x8 slice. The times are simulated.
512 devices in a mesh: seq: 64 (over y, x, core), tp: 8 (over z).
Axes of the slice: x: 4, y: 8, z: 8, core: 2. Of those that a mesh axis runs over, the one named last changes fastest.
Arguments:
- tokens: bfloat16 [16384, 4096], P('seq', 'tp'), may hold values from -30 to 30
- w_qkv: bfloat16 [4096, 3, 2048], P('seq', None, 'tp'), may hold values from -1 to 1
- keep_list: int32 [8192], P('seq'), may hold values from 0 to 255, as said below
- counts: int32 [64], P('seq'), may hold values from 1 to 127, as said below
Outputs:
- attended: bfloat16 [4096, 2048], P('seq', 'tp')
Inputs may be any that keep to these rules, and one draw needn't show every extreme that they name: `counts`: the entries sum to 4096; one shard keeps 2 * 64 - 1 tokens and one shard keeps 1. `keep_list`: entries s * 2 * 64 to s * 2 * 64 + 2 * 64 - 1 are distinct token indices within shard s; the first counts[s] of them increase.
All inputs are finite; a program needn't handle non-finite values.
Results may differ from a plain program's by a relative error of at most 0.0065.
Values may be sent and summed in bfloat16 or wider, within the bound.
A program may use at most 64 MiB of HBM per device.

v0:
```python
import jax
import jax.numpy as jnp
from jax import lax
from jax.sharding import PartitionSpec as P

HD = 128


def entering(value, axis, join, neutral):
    count, mine = (lax.axis_size(axis), lax.axis_index(axis))
    pieces = lax.all_gather(value, axis)
    so_far = jnp.full_like(value, 0) + jnp.asarray(neutral, value.dtype)

    def lap(position, so_far):
        longer = join(so_far, pieces[position])
        return jnp.where(position < mine, longer, so_far)

    return lax.fori_loop(0, count - 1, lap, so_far)


def add_sums(earlier, later):
    return earlier + later


def on_device(tokens, w_qkv, keep_list, counts):
    shards = lax.axis_size("seq")
    my_index = lax.axis_index("seq")
    tok_dev = tokens.shape[0]
    slots = keep_list.shape[0]
    capacity = slots // 2
    per_peer = slots // shards
    head_dim = HD
    columns = w_qkv.shape[2]
    local_heads = columns // head_dim
    offset = entering(counts, "seq", add_sums, jnp.zeros_like(counts))[0]
    peers = jnp.arange(shards, dtype=jnp.int32)[:, None]
    rounds = jnp.arange(per_peer, dtype=jnp.int32)[None, :]
    local_slot = (peers - offset) % shards + rounds * shards
    live = local_slot < counts[0]
    token_index = keep_list[local_slot]
    ranks = jnp.where(live, offset + local_slot, -1).astype(jnp.int32)
    positions = my_index * tok_dev + token_index
    meta = jnp.stack([positions, ranks], axis=2)
    picked = jnp.where(live[:, :, None], tokens[token_index], jnp.zeros((), tokens.dtype))
    arrived, arrived_meta = (
        lax.all_to_all(picked, "seq", split_axis=0, concat_axis=0, tiled=True),
        lax.all_to_all(meta, "seq", split_axis=0, concat_axis=0, tiled=True),
    )
    arrived_meta = arrived_meta.reshape(shards * per_peer, 2)
    arrived_rank = arrived_meta[:, 1]
    target = jnp.where(arrived_rank >= 0, arrived_rank // shards, capacity)
    flat = arrived.reshape(shards * per_peer, arrived.shape[2])
    kept = jnp.zeros((capacity, flat.shape[1]), flat.dtype).at[target].set(flat, mode="drop")
    kept_pos = jnp.zeros((capacity,), jnp.int32).at[target].set(arrived_meta[:, 0], mode="drop")
    full_rows = lax.all_gather(kept, "tp", axis=1, tiled=True)
    piece = lax.all_gather(w_qkv, "seq", axis=0, tiled=True)
    part_rows = lax.slice_in_dim(full_rows, 0, piece.shape[0], axis=1)
    projected = jnp.einsum(
        "rd,dgc->rgc", part_rows, piece, preferred_element_type=jnp.float32
    ).astype(jnp.bfloat16)
    queries = projected[:, 0].reshape(capacity, local_heads, head_dim)
    key_values = projected[:, 1:]
    scale = head_dim ** (-0.5)
    top = jnp.full((local_heads, capacity), -jnp.inf, jnp.float32)
    denom = jnp.zeros((local_heads, capacity), jnp.float32)
    numer = jnp.zeros((local_heads, capacity, head_dim), jnp.float32)
    kv_piece = lax.all_gather(key_values, "seq", axis=0, tiled=True)
    pos_piece = lax.all_gather(kept_pos, "seq", axis=0, tiled=True)
    width = kv_piece.shape[0]
    keys_piece = kv_piece[:, 0].reshape(width, local_heads, head_dim)
    values_piece = kv_piece[:, 1].reshape(width, local_heads, head_dim)
    scores = (
        jnp.einsum("qhd,khd->hqk", queries, keys_piece, preferred_element_type=jnp.float32) * scale
    )
    masked = pos_piece[None, None, :] > kept_pos[None, :, None]
    scores = jnp.where(masked, -jnp.inf, scores)
    new_top = jnp.max(scores, axis=2)
    safe_top = jnp.where(new_top == -jnp.inf, 0.0, new_top)
    expo = jnp.exp(scores - safe_top[..., None])
    shrink = jnp.exp(top - safe_top)
    denom = denom * shrink + jnp.sum(expo, axis=2)
    update = jnp.einsum(
        "hqk,khd->hqd", expo.astype(jnp.bfloat16), values_piece, preferred_element_type=jnp.float32
    )
    numer = numer * shrink[..., None] + update
    top, denom, numer = (new_top, denom, numer)
    result = numer / denom[..., None]
    return jnp.transpose(result, (1, 0, 2)).reshape(capacity, columns).astype(jnp.bfloat16)


def solution(mesh):
    in_specs = (P("seq", "tp"), P("seq", None, "tp"), P("seq"), P("seq"))
    out_specs = P("seq", "tp")
    return jax.shard_map(
        on_device, mesh=mesh, in_specs=in_specs, out_specs=out_specs, check_vma=False
    )
```

profile of v0, /device:TPU:1, one launch (start us, length us, event | category | flops | bytes accessed | tf_op | source)
XLA Modules:
  0.0 447.7 jit_solution(5106883272353101547)
XLA Ops:
  6.5 0.7 all-gather.4.cloned.1.call-update
  7.9 1.3 dynamic-slice
  9.2 0.7 dynamic-update-slice
  10.0 18.3 %all-reduce = s32[64]{0:T(128)S(1)} all-reduce(s32[64]{0:T(128)S(1)} %dynamic-update-slice), channel_id=2, replica_groups=mesh['seq'=64,'tp'=8] {'seq'}, use_global_device_ids=true, to_apply=%add | all-reduce | flops 64 | bytes 512
  28.3 78.4 %while.13 = (s32[]{:T(128)}, s32[1]{0:T(128)}, s32[]{:T(128)}, s32[64,1]{0,1:T(1,128)S(1)}, s32[]{:T(128)}) while((s32[]{:T(128)}, s32[1]{0:T(128)}, s32[]{:T(128)}, s32[64,1]{0,1:T(1,128)S(1)}, s32[]{:T(128)}) %tuple.41), condition=%wide.region_1.2_spmd, body=%wide.region_0.1_spmd.sunk | while | flops 5 | bytes 115 | solution.py:18
  106.9 1.2 gather_fusion
  108.3 0.7 copy.26
  109.0 11.4 %all-to-all-start = ((s32[64,2,2]{1,2,0:T(2,128)}), s32[64,2,2]{1,2,0:T(2,128)S(1)}, u32[]{:S(2)}, u32[]{:S(2)}) async-start(s32[64,2,2]{1,2,0:T(2,128)} %copy.26), calls=%async_computation | async-start | bytes 131072 | tf_op jit(solution)/shard_map/all_to_all | solution.py:47
  120.6 0.8 gather_fusion.1
  121.7 0.9 broadcast_select_fusion
  122.6 7.9 %all-to-all-done = s32[64,2,2]{1,2,0:T(2,128)S(1)} async-done(((s32[64,2,2]{1,2,0:T(2,128)}), s32[64,2,2]{1,2,0:T(2,128)S(1)}, u32[]{:S(2)}, u32[]{:S(2)}) %all-to-all-start) | async-done | bytes 1056 | tf_op jit(solution)/shard_map/all_to_all | solution.py:47
  130.5 4.4 all-to-all-start.1
  135.2 11.1 %all-to-all-done.1 = bf16[64,2,512]{2,1,0:T(2,128)(2,1)S(1)} async-done(((bf16[64,2,512]{2,1,0:T(2,128)(2,1)}), bf16[64,2,512]{2,1,0:T(2,128)(2,1)S(1)}, u32[]{:S(2)}, u32[]{:S(2)}) %all-to-all-start.1) | async-done | bytes 131104 | tf_op jit(solution)/shard_map/all_to_all | solution.py:46
  146.3 1.1 scatter_custom_fusion.1
  147.4 23.8 %all_gather.21 = bf16[64,4096]{1,0:T(8,128)(2,1)S(1)} all-gather(bf16[64,512]{1,0:T(8,128)(2,1)S(1)} %scatter_custom_fusion.1), channel_id=1, replica_groups=mesh['seq'=64,'tp'=8] {'tp'}, dimensions={1}, use_global_device_ids=true | all-gather | bytes 589824 | tf_op jit(solution)/shard_map/all_gather | solution.py:55
  171.2 4.0 convolution_convert_fusion
  176.4 1.0 scatter_custom_fusion
  177.7 247.6 %all-reduce.1 = s32[4096]{0:T(1024)S(1)} all-reduce(s32[4096]{0:T(1024)S(1)} %dynamic-update-slice.1), channel_id=1, replica_groups=mesh['seq'=64,'tp'=8] {'seq'}, use_global_device_ids=true, to_apply=%add.1 | all-reduce | flops 4096 | bytes 32768
  425.5 3.8 fusion.35
  429.3 4.0 reshape_squeeze.11
  433.3 2.0 reshape_squeeze.10
  435.3 2.6 fusion.36
  438.4 1.1 copy-done.2
  439.5 0.7 fusion.18
  (101 shorter events, 40.7 us)
Async XLA Ops:
  6.5 114.1 %copy-start = (bf16[256,512]{1,0:T(8,128)(2,1)S(1)}, bf16[256,512]{1,0:T(8,128)(2,1)}, u32[]{:S(2)}) copy-start(bf16[256,512]{1,0:T(8,128)(2,1)} %param.6) | copy-start | bytes 786436
  6.5 100.4 %copy-start.1 = (s32[128]{0:T(128)S(1)}, s32[128]{0:T(128)}, u32[]{:S(2)}) copy-start(s32[128]{0:T(128)} %param.8) | copy-start | bytes 1540
  6.5 164.6 %all-gather.4.cloned.1.call-start = ((), (), s32[]{:S(2)}) async-start(), calls=%async_computation.2 | async-start | bytes 6389760 | tf_op jit(solution)/shard_map/all_gather | solution.py:56
  109.0 21.5 %all-to-all-start = ((s32[64,2,2]{1,2,0:T(2,128)}), s32[64,2,2]{1,2,0:T(2,128)S(1)}, u32[]{:S(2)}, u32[]{:S(2)}) async-start(s32[64,2,2]{1,2,0:T(2,128)} %copy.26), calls=%async_computation | async-start | bytes 131072 | tf_op jit(solution)/shard_map/all_to_all | solution.py:47
  130.5 15.8 %all-to-all-start.1 = ((bf16[64,2,512]{2,1,0:T(2,128)(2,1)}), bf16[64,2,512]{2,1,0:T(2,128)(2,1)S(1)}, u32[]{:S(2)}, u32[]{:S(2)}) async-start(bf16[64,2,512]{2,1,0:T(2,128)(2,1)} %broadcast_select_fusion), calls=%async_computation.1 | async-start | bytes 262144 | tf_op jit(solution)/shard_map/all_to_all | solution.py:46
  134.9 290.6 %all-gather.6.cloned.1.call-start = ((), (), s32[]{:S(2)}) async-start(), calls=%async_computation.3 | async-start | bytes 4259840 | tf_op jit(solution)/shard_map/all_gather | solution.py:67
  437.9 1.6 copy-start.2
Sparse Core Ops, SparseCore 0:
  10.8 92.2 all-gather.3
  175.9 82.4 all-gather.5
where the time goes:
time: 454 us; the launch traced here: 448 us
  blocking collectives  290 us (64%)
  local copies, waits for them, and re-layouts  57.5 us (13%)
  loops' own time  41 us (9%)
  waiting for transfers between devices  19.8 us (4%)
  starting transfers between devices  15.9 us (4%)
  between operations  14.9 us (3%)
  matrix products  7.24 us (2%)
    unnamed x2, blocking collectives  266 us
    another operation x1, loops' own time, entering(): return lax.fori_loop(0, count - 1, lap, so_far)  41 us
    dynamic_slice x63, local copies, waits for them, and re-layouts, lap(): longer = join(so_far, pieces[position])  37.4 us
    all_gather x1, blocking collectives, on_device(): full_rows = lax.all_gather(kept, 'tp', axis=1, tiled=True)  23.8 us
    all_to_all x1, starting transfers between devices, on_device(): lax.all_to_all(meta, 'seq', split_axis=0, concat_axis=0, tiled=True)  11.4 us
    all_to_all x1, waiting for transfers between devices, on_device(): lax.all_to_all(picked, 'seq', split_axis=0, concat_axis=0, tiled=True)  11.1 us
  transfers between devices with their start and end apart: 4, of which 2 were waited for; matrix products, arithmetic and copies ran while one was open for 10% of the time, Pallas kernels for 0%

commit v1 on v0

v1 whole, which is shorter than its diff:
```python
import math

import jax
import jax.numpy as jnp
from jax import lax
from jax.experimental import pallas as pl
from jax.experimental.pallas import tpu as pltpu
from jax.sharding import PartitionSpec as P

MESH = pl.DeviceIdType.MESH
NX, NY, NZ = 4, 8, 8
HD = 128
BF = jnp.bfloat16
F32 = jnp.float32
SEMS = 220


class Links:
    def __init__(self, send_sem, recv_sem):
        self.send_sem, self.recv_sem, self.count, self.copies = send_sem, recv_sem, 0, []

    def send(self, src, dst, device):
        copy = pltpu.make_async_remote_copy(
            src_ref=src,
            dst_ref=dst,
            send_sem=self.send_sem.at[self.count],
            recv_sem=self.recv_sem.at[self.count],
            device_id=device,
            device_id_type=MESH,
        )
        self.count += 1
        copy.start()
        self.copies.append(copy)
        return copy

    def drain(self):
        for copy in self.copies:
            copy.wait_send()


class Gather:
    def __init__(self, links, buf, place):
        self.links, self.buf = links, buf
        self.x, self.y, self.dev = place
        self.xp, self.xm, self.x2 = [(self.x + k) % NX for k in (1, 3, 2)]

    def row(self, k):
        return (self.y + k + NY) % NY

    def put(self, y, x, rows, to):
        lo, hi = rows
        piece = self.buf.at[y, pl.ds(0, NX) if x is None else x, pl.ds(lo, hi - lo)]
        ty, tx = to
        return self.links.send(piece, piece, self.dev(ty, tx))

    def along_x(self, y, x, rows):
        return (self.put(y, x, rows, (self.y, self.xp)), self.put(y, x, rows, (self.y, self.xm)))

    def steps(self):
        one, two = (0, 48), (48, 128)
        one_a, one_b, two_a, two_b = (0, 32), (32, 48), (48, 96), (96, 128)
        x, y, xp, xm, x2 = self.x, self.y, self.xp, self.xm, self.x2
        up, down = (self.row(1), x), (self.row(-1), x)

        def arrive(copies):
            for copy in copies:
                copy.wait_recv()

        def both_y(chunk, rows):
            return [self.put(y, chunk, rows, up), self.put(y, chunk, rows, down)]

        def on_y(k, chunk, rows_a, rows_b):
            return [
                self.put(self.row(1 - k), chunk, rows_a, up),
                self.put(self.row(k - 1), chunk, rows_b, down),
            ]

        def on_x(rows_list):
            done = []
            for r in rows_list:
                done += self.along_x(r, x, two)
            return done

        def half_x(rows_list):
            done = []
            for r in rows_list:
                done.append(self.put(r, xm, two_a, (y, xp)))
                done.append(self.put(r, xp, two_b, (y, xm)))
            return done

        first = self.along_x(y, x, one)
        ys = {1: on_y(1, x, two, two)}
        xs = {0: on_x([y])}
        tall = {1: both_y(x, one)}
        late = []
        yield
        arrive(ys[1])
        ys[2] = on_y(2, x, two, two)
        xs[1] = on_x([self.row(-1), self.row(1)])
        yield
        arrive(first)
        half = [self.put(y, xm, one_a, (y, xp)), self.put(y, xp, one_b, (y, xm))]
        tall[1] += both_y(xm, one) + both_y(xp, one)
        yield
        arrive(xs[0])
        late += half_x([y])
        yield
        arrive(ys[2])
        ys[3] = on_y(3, x, two, two)
        xs[2] = on_x([self.row(-2), self.row(2)])
        yield
        arrive(half)
        tall[1] += both_y(x2, one)
        yield
        arrive(tall[1])
        tall[2] = on_y(2, None, one, one)
        yield
        arrive(ys[3])
        ys[4] = on_y(4, x, two_a, two_b)
        xs[3] = on_x([self.row(-3), self.row(3)])
        yield
        arrive(xs[1])
        late += half_x([self.row(-1), self.row(1)])
        yield
        arrive(ys[4])
        xs[4] = on_x([self.row(4)])
        yield
        arrive(tall[2])
        tall[3] = on_y(3, None, one, one)
        yield
        arrive(xs[2])
        late += half_x([self.row(-2), self.row(2)])
        yield
        arrive(tall[3])
        tall[4] = on_y(4, None, one_a, one_b)
        yield
        arrive(xs[3])
        late += half_x([self.row(-3), self.row(3)])
        yield
        arrive(xs[4])
        late += half_x([self.row(4)])
        yield
        arrive(tall[4] + late)
        yield


def iota(shape, axis):
    return lax.broadcasted_iota(jnp.int32, shape, axis)


def pick(mask, rows):
    ones = jnp.where(mask, 1.0, 0.0).astype(BF)
    return jnp.dot(ones, rows, preferred_element_type=F32).astype(BF)


def kernel(
    tokens, w, keep, count, out,
    wbuf, kv, feats, cbuf, slots, send1, recv1, send2, recv2, scores, heads, fin,
    send_sem, recv_sem, local_sem,
):
    s, z = lax.axis_index("seq"), lax.axis_index("tp")
    c = s % 2
    x = (s // 2) % NX
    y = s // (2 * NX)
    chip = s // 2
    e = s % 8

    def dev(yy, xx):
        return ((yy * NX + xx) * 2 + c, z)

    sibling = (s + 1 - 2 * c, z)
    y_peers = [(y + k) % NY for k in range(1, NY)]
    row_peers = [(e + k) % 8 for k in range(1, 8)]
    z_order = (1, 7, 2, 6, 3, 5, 4)
    z_peers = [(z + k) % NZ for k in z_order]

    barrier = pltpu.get_barrier_semaphore()
    greet = [(p * 8 + e, z) for p in y_peers]
    greet += [(y * 8 + p, z) for p in row_peers]
    greet += [(s, p) for p in z_peers]
    for device in greet:
        pl.semaphore_signal(barrier, inc=1, device_id=device, device_id_type=MESH)
    cbuf[y, e] = jnp.full((1, 128), count[0], jnp.int32)
    pl.semaphore_wait(barrier, len(greet))

    links = Links(send_sem, recv_sem)

    counts1 = [
        links.send(cbuf.at[y, e], cbuf.at[y, e], (y * 8 + p, z)) for p in row_peers
    ]

    mine, other = pl.multiple_of(c * HD, HD), pl.multiple_of((1 - c) * HD, HD)
    half = pl.ds(pl.multiple_of(c * 64, 64), 64)
    swap, local = [], []
    for g in range(3):
        place = wbuf.at[y, x, half, pl.ds(g * HD, HD)]
        swap.append(links.send(w.at[g, :, pl.ds(other, HD)], place, sibling))
        local.append(
            pltpu.make_async_copy(w.at[g, :, pl.ds(mine, HD)], place, local_sem.at[g])
        )
        local[-1].start()

    chosen = (iota((256, 128), 0) == keep[...]).astype(F32).astype(BF)
    slots[...] = lax.dot_general(
        chosen, tokens[...], (((0,), (0,)), ((), ())), preferred_element_type=F32
    ).astype(BF)

    for copy in local:
        copy.wait()
    for copy in swap:
        copy.wait_recv()
    gather = Gather(links, wbuf, (x, y, dev)).steps()
    next(gather)

    for copy in counts1:
        copy.wait_recv()
    counts2 = [links.send(cbuf.at[y], cbuf.at[y], (p * 8 + e, z)) for p in y_peers]
    next(gather)
    for copy in counts2:
        copy.wait_recv()

    counts = cbuf[...].reshape(64, 128)
    shard = iota((64, 128), 0)
    start = jnp.sum(jnp.where(shard < s, counts, 0), axis=0, keepdims=True)
    total = jnp.sum(jnp.where(shard == s, counts, 0), axis=0, keepdims=True)
    r, i = iota((128, 128), 0), iota((128, 128), 1)
    hit = (r // 2 == (start + i) % 64) & (r % 2 == i // 64) & (i < total)
    send1[...] = pick(hit, slots[...]).reshape(8, 16, 512)
    stage1 = [links.send(send1.at[p], recv1.at[y], (p * 8 + e, z)) for p in y_peers]
    own1 = pltpu.make_async_copy(send1.at[y], recv1.at[y], local_sem.at[3])
    own1.start()
    next(gather)
    next(gather)
    own1.wait()
    for copy in stage1:
        copy.wait_recv()
    turn = (r // 16 == (i // 2) % 8) & ((r // 2) % 8 == i // 16) & (r % 2 == i % 2)
    send2[...] = pick(turn, recv1[...].reshape(128, 512)).reshape(8, 16, 512)
    stage2 = [links.send(send2.at[p], recv2.at[e], (y * 8 + p, z)) for p in row_peers]
    own2 = pltpu.make_async_copy(send2.at[e], recv2.at[e], local_sem.at[4])
    own2.start()
    next(gather)
    next(gather)
    own2.wait()
    for copy in stage2:
        copy.wait_recv()
    lane = iota((64, 128), 1)
    source = ((lane // 2) % 8) * 8 + lane // 16
    begin = jnp.sum(jnp.where(shard < source, counts, 0), axis=0, keepdims=True)
    size = jnp.sum(jnp.where(shard == source, counts, 0), axis=0, keepdims=True)
    within = shard * 64 + s - begin
    live = (within >= 0) & (within < size) & ((within >= 64) == (lane % 2 == 1))
    feats[z, c] = pick(live, recv2[...].reshape(128, 512))

    over_z = [links.send(feats.at[z, c], feats.at[z, c], (s, p)) for p in z_peers]
    beside = [links.send(feats.at[z, c], feats.at[z, c], sibling)]
    for _ in range(3):
        next(gather)
    for k, copy in zip(z_order, over_z):
        copy.wait_recv()
        piece = feats.at[(z - k + NZ) % NZ, c]
        beside.append(links.send(piece, piece, sibling))
        if k in (7, 6, 5):
            next(gather)
    for _ in gather:
        pass
    for copy in beside:
        copy.wait_recv()

    def project(zz, acc):
        rows = feats[zz].reshape(128, 512)
        return acc + jnp.dot(rows, wbuf[zz].reshape(512, 384), preferred_element_type=F32)

    acc = lax.fori_loop(0, NZ, project, jnp.zeros((128, 384), F32))
    query = acc[:, :HD].astype(BF)
    kv[y, x] = acc[:, HD:].astype(BF)

    for _ in Gather(links, kv, (x, y, dev)).steps():
        pass

    qi, kj = iota((128, 512), 0), iota((128, 512), 1)
    rank_q = (qi % 64) * 64 + chip * 2 + qi // 64
    rank_k = (kj % 64) * 64 + (kj // 128) * 2 + (kj // 64) % 2
    scale = HD ** (-0.5)

    def score(yy, top):
        keys = kv[yy, :, :, :HD].reshape(512, HD)
        dots = lax.dot_general(
            query, keys, (((1,), (1,)), ((), ())), preferred_element_type=F32
        ) * scale
        dots = jnp.where(rank_k + yy * 8 > rank_q, -jnp.inf, dots)
        scores[yy] = dots
        return jnp.maximum(top, jnp.max(dots, axis=1, keepdims=True))

    top = lax.fori_loop(0, NY, score, jnp.full((128, 1), -jnp.inf, F32))

    def weigh(yy, carry):
        denom, numer = carry
        expo = jnp.exp(scores[yy] - top)
        values = kv[yy, :, :, HD:].reshape(512, HD)
        numer = numer + jnp.dot(expo.astype(BF), values, preferred_element_type=F32)
        return denom + jnp.sum(expo, axis=1, keepdims=True), numer

    denom, numer = lax.fori_loop(
        0, NY, weigh, (jnp.zeros((128, 1), F32), jnp.zeros((128, HD), F32))
    )
    heads[...] = (numer / denom).astype(BF).reshape(2, 64, HD)

    last = links.send(heads.at[1 - c], fin.at[c], sibling)
    own = pltpu.make_async_copy(heads.at[c], fin.at[c], local_sem.at[5])
    own.start()
    own.wait()
    last.wait_recv()
    out[:, :HD] = fin[0]
    out[:, HD:] = fin[1]
    links.drain()


def on_device(tokens, w_qkv, keep_list, counts):
    vmem = pl.BlockSpec(memory_space=pltpu.VMEM)
    return pl.pallas_call(
        kernel,
        out_shape=jax.ShapeDtypeStruct((64, 256), BF),
        in_specs=[
            vmem,
            pl.BlockSpec(memory_space=pl.ANY),
            vmem,
            pl.BlockSpec(memory_space=pltpu.SMEM),
        ],
        out_specs=vmem,
        scratch_shapes=[
            pltpu.VMEM((NY, NX, 128, 384), BF),
            pltpu.VMEM((NY, NX, 128, 256), BF),
            pltpu.VMEM((NZ, 2, 64, 512), BF),
            pltpu.VMEM((8, 8, 1, 128), jnp.int32),
            pltpu.VMEM((128, 512), BF),
            pltpu.VMEM((8, 16, 512), BF),
            pltpu.VMEM((8, 16, 512), BF),
            pltpu.VMEM((8, 16, 512), BF),
            pltpu.VMEM((8, 16, 512), BF),
            pltpu.VMEM((8, 128, 512), F32),
            pltpu.VMEM((2, 64, HD), BF),
            pltpu.VMEM((2, 64, HD), BF),
            pltpu.SemaphoreType.DMA((SEMS,)),
            pltpu.SemaphoreType.DMA((SEMS,)),
            pltpu.SemaphoreType.DMA((8,)),
        ],
        compiler_params=pltpu.CompilerParams(
            collective_id=0, has_side_effects=True, vmem_limit_bytes=48 * 1024 * 1024
        ),
    )(tokens, jnp.transpose(w_qkv, (1, 0, 2)), keep_list.reshape(1, 128), counts)


def solution(mesh):
    in_specs = (P("seq", "tp"), P("seq", None, "tp"), P("seq"), P("seq"))
    return jax.shard_map(
        on_device, mesh=mesh, in_specs=in_specs, out_specs=P("seq", "tp"), check_vma=False
    )
```

time: 454 us -> 93.5 us (0.21); the launches traced: 448 us -> 93.3 us
  blocking collectives: 290 us -> 0 us
  Pallas kernels: 0 us -> 89.5 us
  local copies, waits for them, and re-layouts: 57.5 us -> 3.11 us
  loops' own time: 41 us -> 0 us
  waiting for transfers between devices: 19.8 us -> 0 us
  starting transfers between devices: 15.9 us -> 0 us
  between operations: 14.9 us -> 0.67 us
  matrix products: 7.24 us -> 0 us
    unnamed x2 -> x0, blocking collectives: 266 us -> none
    pallas_call x0 -> x1, Pallas kernels: none -> 89.5 us  [on_device(): pl.pallas_call(kernel, out_shape=jax.ShapeDtypeStruct((64, 256), BF), in_...]
    another operation x1 -> x0, loops' own time: 41 us -> none  [entering(): return lax.fori_loop(0, count - 1, lap, so_far)]
    dynamic_slice x63 -> x0, local copies, waits for them, and re-layouts: 37.4 us -> none  [lap(): longer = join(so_far, pieces[position])]
    all_gather x1 -> x0, blocking collectives: 23.8 us -> none  [on_device(): full_rows = lax.all_gather(kept, 'tp', axis=1, tiled=True)]
    all_to_all x2 -> x0, waiting for transfers between devices: 19.1 us -> none  [the longest x1 11.1 us: on_device(): lax.all_to_all(picked, 'seq', split_axis=0, concat_axis=0, tiled=True)]
    all_to_all x2 -> x0, starting transfers between devices: 15.8 us -> none  [the longest x1 11.4 us: on_device(): lax.all_to_all(meta, 'seq', split_axis=0, concat_axis=0, tiled=True)]
    dot_general x3 -> x0, matrix products: 7.24 us -> none  [the longest x1 3.97 us: on_device(): jnp.einsum('rd,dgc->rgc', part_rows, piece, preferred_element_type=jnp.fl...]
  transfers between devices with their start and end apart: 4 -> 0, of which waited for: 2 -> 0; matrix products, arithmetic and copies ran while one was open for 10% -> 0% of each run, Pallas kernels for 0% -> 0%
where the time goes in v1:
time: 93.5 us; the launch traced here: 93.3 us
  Pallas kernels  89.5 us (96%)
  local copies, waits for them, and re-layouts  3.11 us (3%)
    pallas_call x1, Pallas kernels, on_device(): pl.pallas_call(kernel, out_shape=jax.ShapeDtypeStruct((64, 256), BF), in_...  89.5 us
    unnamed x7, local copies, waits for them, and re-layouts  3.11 us

profile of v1, /device:TPU:1, one launch (start us, length us, event | category | flops | bytes accessed | tf_op | source)
XLA Modules:
  0.0 93.3 jit_solution(7952695070941671888)
XLA Ops:
  0.7 0.0 copy-start.2
  0.7 0.6 copy-done.2
  1.3 0.0 copy-start
  1.3 0.9 %copy-done = bf16[256,512]{1,0:T(8,128)(2,1)S(1)} copy-done((bf16[256,512]{1,0:T(8,128)(2,1)S(1)}, bf16[256,512]{1,0:T(8,128)(2,1)}, u32[]{:S(2)}) %copy-start) | copy-done | bytes 262168
  2.3 0.0 copy-start.1
  2.3 0.9 copy-done.1
  3.2 89.5 %shard_map.46 = bf16[64,256]{1,0:T(8,128)(2,1)S(1)} custom-call(bf16[256,512]{1,0:T(8,128)(2,1)S(1)} %copy-done, bf16[3,64,256]{2,1,0:T(8,128)(2,1)S(1)} %bitcast.2, s32[1,128]{1,0:T(1,128)S(1)} %bitcast.3, s32[1]{0:T(128)S(6)} %copy.6.count), custom_call_target="tpu_custom_call" | custom-call | tf_op jit(solution)/shard_map/pallas_call | solution.py:321
  92.7 0.6 copy.7
Async XLA Ops:
  0.7 0.7 copy-start.2
  1.3 0.9 %copy-start = (bf16[256,512]{1,0:T(8,128)(2,1)S(1)}, bf16[256,512]{1,0:T(8,128)(2,1)}, u32[]{:S(2)}) copy-start(bf16[256,512]{1,0:T(8,128)(2,1)} %tokens.1) | copy-start | bytes 786436
  2.3 0.9 copy-start.1

commit v2 on v0

v2 whole, which is shorter than its diff:
```python
import heapq

import jax
import jax.numpy as jnp
from jax import lax
from jax.experimental import pallas as pl
from jax.experimental.pallas import tpu as pltpu
from jax.sharding import PartitionSpec as P

MESH = pl.DeviceIdType.MESH
NX, NY, NZ = 4, 8, 8
HD = 128
BF = jnp.bfloat16
F32 = jnp.float32
I32 = jnp.int32
SEMS = 352
PEERS = sorted(
    ((dy, dx, dc) for dy in range(NY) for dx in range(NX) for dc in range(2) if dy or dx or dc),
    key=lambda p: -min(p[0], NY - p[0]) - min(p[1], NX - p[1]),
)


class Links:
    def __init__(self, send_sem, recv_sem):
        self.send_sem, self.recv_sem, self.count, self.copies = send_sem, recv_sem, 0, []

    def send(self, src, dst, device):
        copy = pltpu.make_async_remote_copy(
            src_ref=src,
            dst_ref=dst,
            send_sem=self.send_sem.at[self.count],
            recv_sem=self.recv_sem.at[self.count],
            device_id=device,
            device_id_type=MESH,
        )
        self.count += 1
        copy.start()
        self.copies.append(copy)
        return copy

    def drain(self):
        for copy in self.copies:
            copy.wait_send()


class Gather:
    ONE, ONE_A, ONE_B = (0, 48), (0, 32), (32, 48)
    TWO, TWO_A, TWO_B = (48, 128), (48, 96), (96, 128)

    def __init__(self, links, buf, place, unit):
        self.links, self.buf, self.unit = links, buf, unit
        self.x, self.y, self.dev = place
        self.clock, self.busy, self.queue, self.number = 0.0, {}, [], 0

    def col(self, k):
        return (self.x + k + NX) % NX

    def row(self, k):
        return (self.y + k + NY) % NY

    def send(self, row, col, rows, step):
        lo, hi = rows
        piece = self.buf.at[self.row(row), self.col(col), pl.ds(lo, hi - lo)]
        sy, sx = step
        copy = self.links.send(piece, piece, self.dev(self.row(sy), self.col(sx)))
        self.clock += 0.06
        hops = abs(sy) + abs(sx)
        way = (sy > 0, sy < 0, sx > 0, sx < 0)
        end = max(self.busy.get(way, 0.0), self.clock) + (hi - lo) / 128 * self.unit * hops
        self.busy[way] = end
        return copy, end + 1.95 + 0.65 * hops

    def when(self, sent, then):
        self.number += 1
        entry = (max(t for _, t in sent), self.number, [copy for copy, _ in sent], then)
        heapq.heappush(self.queue, entry)

    def advance(self, until):
        while self.queue and self.queue[0][0] <= until:
            at, _, copies, then = heapq.heappop(self.queue)
            for copy in copies:
                copy.wait_recv()
            self.clock = max(self.clock, at)
            then()

    def finish(self):
        self.advance(1e9)

    def ring_y(self, col, k=0):
        up = self.ONE_A if k == 3 else self.ONE
        down = self.ONE_B if k == 3 else self.ONE
        sent = [self.send(-k, col, up, (1, 0)), self.send(k, col, down, (-1, 0))]
        self.when(sent, (lambda: self.ring_y(col, k + 1)) if k < 3 else (lambda: None))

    def tree_y(self):
        far = [self.send(0, 0, self.TWO, (2, 0)), self.send(0, 0, self.TWO, (-2, 0))]
        near = [self.send(0, 0, self.TWO, (1, 0)), self.send(0, 0, self.TWO, (-1, 0))]

        def arrived():
            last = [self.send(-2, 0, self.TWO_A, (2, 0)), self.send(2, 0, self.TWO_B, (-2, 0))]
            third = [self.send(-2, 0, self.TWO, (1, 0)), self.send(2, 0, self.TWO, (-1, 0))]
            self.when(third, lambda: self.ring_x((-3, 3)))
            self.when(last, lambda: self.ring_x((4,)))
            self.ring_x((-2, 2))

        self.when(near, lambda: self.ring_x((-1, 1)))
        self.when(far, arrived)

    def ring_x(self, rows):
        sent = []
        for r in rows:
            sent += [self.send(r, 0, self.TWO, (0, 1)), self.send(r, 0, self.TWO, (0, -1))]

        def arrived():
            rest = []
            for r in rows:
                rest += [self.send(r, -1, self.TWO_A, (0, 1)), self.send(r, 1, self.TWO_B, (0, -1))]
            self.when(rest, lambda: None)

        self.when(sent, arrived)

    def start(self):
        sent = [self.send(0, 0, self.ONE, (0, 1)), self.send(0, 0, self.ONE, (0, -1))]

        def arrived():
            rest = [self.send(0, -1, self.ONE_A, (0, 1)), self.send(0, 1, self.ONE_B, (0, -1))]
            self.when(rest, lambda: self.ring_y(2))
            self.ring_y(-1)
            self.ring_y(1)

        self.when(sent, arrived)
        self.tree_y()
        self.ring_x((0,))
        self.ring_y(0)


def iota(shape, axis):
    return lax.broadcasted_iota(I32, shape, axis)


def pick(mask, rows):
    ones = jnp.where(mask, 1.0, 0.0).astype(BF)
    return jnp.dot(ones, rows, preferred_element_type=F32).astype(BF)


def kernel(
    tokens_hbm, w, keep_hbm, count_hbm, out,
    tokens, keep, count, wbuf, kv, feats, cbuf, slots, outbox, inbox, scores, heads, fin,
    send_sem, recv_sem, local_sem,
):
    s, z = lax.axis_index("seq"), lax.axis_index("tp")
    c = s % 2
    x = (s // 2) % NX
    y = s // (2 * NX)
    chip = s // 2

    def dev(yy, xx):
        return ((yy * NX + xx) * 2 + c, z)

    sibling = (s + 1 - 2 * c, z)
    peers = [(((y + p) % NY) * NX + (x + q) % NX) * 2 + (c + r) % 2 for p, q, r in PEERS]
    above = [(z + k) % NZ for k in range(NZ)]

    barrier = pltpu.get_barrier_semaphore()
    greet = [(p, z) for p in peers] + [(s, p) for p in above[1:]]
    for device in greet:
        pl.semaphore_signal(barrier, inc=1, device_id=device, device_id_type=MESH)

    mine, other = pl.multiple_of(c * HD, HD), pl.multiple_of((1 - c) * HD, HD)
    half = pl.ds(pl.multiple_of(c * 64, 64), 64)
    place = [wbuf.at[y, x, half, pl.ds(g * HD, HD)] for g in range(3)]
    local = [
        pltpu.make_async_copy(count_hbm, count, local_sem.at[0]),
        pltpu.make_async_copy(keep_hbm, keep, local_sem.at[1]),
        pltpu.make_async_copy(tokens_hbm, tokens, local_sem.at[2]),
    ]
    for g in range(3):
        local.append(
            pltpu.make_async_copy(w.at[g, :, pl.ds(mine, HD)], place[g], local_sem.at[3 + g])
        )
    for copy in local:
        copy.start()
    for copy in local:
        copy.wait()
    cbuf[s] = jnp.full((1, 128), count[0], I32)
    chosen = (iota((256, 128), 0) == keep[...]).astype(F32).astype(BF)
    rows = lax.dot_general(
        chosen, tokens[...], (((0,), (0,)), ((), ())), preferred_element_type=F32
    ).astype(BF)
    for q in range(4):
        slots[q * 128 : (q + 1) * 128] = rows[:, q * 128 : (q + 1) * 128]
    pl.semaphore_wait(barrier, len(greet))

    links = Links(send_sem, recv_sem)
    told = [links.send(cbuf.at[s], cbuf.at[s], (p, z)) for p in peers]
    swap = [links.send(w.at[g, :, pl.ds(other, HD)], place[g], sibling) for g in range(3)]
    for copy in swap:
        copy.wait_recv()
    gather = Gather(links, wbuf, (x, y, dev), 1.97)
    gather.start()
    gather.advance(3.5)
    for copy in told:
        copy.wait_recv()

    counts = cbuf[...].reshape(64, 128)
    shard = iota((64, 128), 0)
    begin = jnp.sum(jnp.where(shard < s, counts, 0), axis=0, keepdims=True)
    total = jnp.sum(jnp.where(shard == s, counts, 0), axis=0, keepdims=True)
    i = iota((1, 128), 1)
    code = jnp.where(i < total, ((begin + i) & 63) * 8 + (i >> 6), -8)
    code = jnp.concatenate([code + q * 2 for q in range(4)], axis=1)
    outbox[...] = pick(iota((512, 512), 0) == code, slots[...]).reshape(64, 8, 128)
    post = [links.send(outbox.at[p], inbox.at[s], (p, z)) for p in peers]
    own = pltpu.make_async_copy(outbox.at[s], inbox.at[s], local_sem.at[6])
    own.start()
    gather.advance(12.0)
    own.wait()
    wide = jnp.concatenate([counts] * 4, axis=1)
    shard, lane = iota((64, 512), 0), iota((64, 512), 1)
    begin = jnp.sum(jnp.where(shard < (lane >> 3), wide, 0), axis=0, keepdims=True)
    size = jnp.sum(jnp.where(shard == (lane >> 3), wide, 0), axis=0, keepdims=True)
    within = shard * 64 + s - begin
    live = (within >= 0) & (within < size) & ((within >> 6) == (lane & 1))
    block = (lane >> 1) & 3
    take = jnp.concatenate([live & (block == q) for q in range(4)], axis=0)
    for copy in post:
        copy.wait_recv()
    kept = pick(take, inbox[...].reshape(512, 128))
    feats[z, c] = jnp.concatenate([kept[q * 64 : (q + 1) * 64] for q in range(4)], axis=1)

    def over_z(k, lo, hi, step):
        piece = feats.at[above[k % NZ], c, pl.ds(lo, hi - lo)]
        return links.send(piece, piece, (s, above[step % NZ]))

    beside = {}

    def hand(k):
        piece = feats.at[above[k % NZ], c]
        beside[k] = links.send(piece, piece, sibling)

    pair2 = [over_z(0, 0, 64, 2), over_z(0, 0, 64, -2)]
    pair1 = [over_z(0, 0, 64, 1), over_z(0, 0, 64, -1)]
    hand(0)
    gather.advance(18.0)
    for copy in pair2:
        copy.wait_recv()
    pair4 = [over_z(-2, 0, 32, 2), over_z(2, 32, 64, -2)]
    pair3 = [over_z(-2, 0, 64, 1), over_z(2, 0, 64, -1)]
    hand(-2)
    hand(2)
    for copy in pair1:
        copy.wait_recv()
    hand(-1)
    hand(1)
    gather.finish()

    acc = jnp.zeros((128, 384), F32)

    def project(acc, k):
        beside[k].wait_recv()
        zz = above[k % NZ]
        block = feats[zz].reshape(128, 512)
        return acc + jnp.dot(block, wbuf[zz].reshape(512, 384), preferred_element_type=F32)

    for k in (0, -2, 2, -1, 1):
        acc = project(acc, k)
    for copy in pair3:
        copy.wait_recv()
    hand(-3)
    hand(3)
    for copy in pair4:
        copy.wait_recv()
    hand(4)
    for k in (-3, 3, 4):
        acc = project(acc, k)
    query = acc[:, :HD].astype(BF)
    kv[y, x] = acc[:, HD:].astype(BF)

    gather = Gather(links, kv, (x, y, dev), 1.31)
    gather.start()
    gather.finish()

    qi, kj = iota((128, 512), 0), iota((128, 512), 1)
    rank_q = (qi & 63) * 64 + chip * 2 + (qi >> 6)
    rank_k = (kj & 63) * 64 + (kj >> 7) * 2 + ((kj >> 6) & 1)
    scale = HD ** (-0.5)

    def score(yy, top):
        keys = kv[yy, :, :, :HD].reshape(512, HD)
        dots = lax.dot_general(
            query, keys, (((1,), (1,)), ((), ())), preferred_element_type=F32
        ) * scale
        dots = jnp.where(rank_k + yy * 8 > rank_q, -jnp.inf, dots)
        scores[yy] = dots
        return jnp.maximum(top, jnp.max(dots, axis=1, keepdims=True))

    top = lax.fori_loop(0, NY, score, jnp.full((128, 1), -jnp.inf, F32))

    def weigh(yy, carry):
        denom, numer = carry
        expo = jnp.exp(scores[yy] - top)
        values = kv[yy, :, :, HD:].reshape(512, HD)
        numer = numer + jnp.dot(expo.astype(BF), values, preferred_element_type=F32)
        return denom + jnp.sum(expo, axis=1, keepdims=True), numer

    denom, numer = lax.fori_loop(
        0, NY, weigh, (jnp.zeros((128, 1), F32), jnp.zeros((128, HD), F32))
    )
    heads[...] = (numer / denom).astype(BF).reshape(2, 64, HD)

    last = links.send(heads.at[1 - c], fin.at[c], sibling)
    own = pltpu.make_async_copy(heads.at[c], fin.at[c], local_sem.at[7])
    own.start()
    own.wait()
    last.wait_recv()
    out[:, :HD] = fin[0]
    out[:, HD:] = fin[1]
    links.drain()


def on_device(tokens, w_qkv, keep_list, counts):
    hbm = pl.BlockSpec(memory_space=pltpu.HBM)
    return pl.pallas_call(
        kernel,
        out_shape=jax.ShapeDtypeStruct((64, 256), BF),
        in_specs=[hbm] * 4,
        out_specs=pl.BlockSpec(memory_space=pltpu.VMEM),
        scratch_shapes=[
            pltpu.VMEM((256, 512), BF),
            pltpu.VMEM((1, 128), I32),
            pltpu.SMEM((1,), I32),
            pltpu.VMEM((NY, NX, 128, 384), BF),
            pltpu.VMEM((NY, NX, 128, 256), BF),
            pltpu.VMEM((NZ, 2, 64, 512), BF),
            pltpu.VMEM((64, 1, 128), I32),
            pltpu.VMEM((512, 128), BF),
            pltpu.VMEM((64, 8, 128), BF),
            pltpu.VMEM((64, 8, 128), BF),
            pltpu.VMEM((8, 128, 512), F32),
            pltpu.VMEM((2, 64, HD), BF),
            pltpu.VMEM((2, 64, HD), BF),
            pltpu.SemaphoreType.DMA((SEMS,)),
            pltpu.SemaphoreType.DMA((SEMS,)),
            pltpu.SemaphoreType.DMA((8,)),
        ],
        compiler_params=pltpu.CompilerParams(
            collective_id=0, has_side_effects=True, vmem_limit_bytes=60 * 1024 * 1024
        ),
    )(tokens, jnp.transpose(w_qkv, (1, 0, 2)), keep_list.reshape(1, 128), counts)


def solution(mesh):
    in_specs = (P("seq", "tp"), P("seq", None, "tp"), P("seq"), P("seq"))
    return jax.shard_map(
        on_device, mesh=mesh, in_specs=in_specs, out_specs=P("seq", "tp"), check_vma=False
    )
```

time: 454 us -> 81 us (0.18); the launches traced: 448 us -> 80.8 us
  blocking collectives: 290 us -> 0 us
  Pallas kernels: 0 us -> 78.8 us
  local copies, waits for them, and re-layouts: 57.5 us -> 1.38 us
  loops' own time: 41 us -> 0 us
  waiting for transfers between devices: 19.8 us -> 0 us
  starting transfers between devices: 15.9 us -> 0 us
  between operations: 14.9 us -> 0.66 us
  matrix products: 7.24 us -> 0 us
    unnamed x2 -> x0, blocking collectives: 266 us -> none
    pallas_call x0 -> x1, Pallas kernels: none -> 78.8 us  [on_device(): pl.pallas_call(kernel, out_shape=jax.ShapeDtypeStruct((64, 256), BF), in_...]
    another operation x1 -> x0, loops' own time: 41 us -> none  [entering(): return lax.fori_loop(0, count - 1, lap, so_far)]
    dynamic_slice x63 -> x0, local copies, waits for them, and re-layouts: 37.4 us -> none  [lap(): longer = join(so_far, pieces[position])]
    all_gather x1 -> x0, blocking collectives: 23.8 us -> none  [on_device(): full_rows = lax.all_gather(kept, 'tp', axis=1, tiled=True)]
    all_to_all x2 -> x0, waiting for transfers between devices: 19.1 us -> none  [the longest x1 11.1 us: on_device(): lax.all_to_all(picked, 'seq', split_axis=0, concat_axis=0, tiled=True)]
    all_to_all x2 -> x0, starting transfers between devices: 15.8 us -> none  [the longest x1 11.4 us: on_device(): lax.all_to_all(meta, 'seq', split_axis=0, concat_axis=0, tiled=True)]
    dot_general x3 -> x0, matrix products: 7.24 us -> none  [the longest x1 3.97 us: on_device(): jnp.einsum('rd,dgc->rgc', part_rows, piece, preferred_element_type=jnp.fl...]
  transfers between devices with their start and end apart: 4 -> 0, of which waited for: 2 -> 0; matrix products, arithmetic and copies ran while one was open for 10% -> 0% of each run, Pallas kernels for 0% -> 0%
where the time goes in v2:
time: 81 us; the launch traced here: 80.8 us
  Pallas kernels  78.8 us (97%)
  local copies, waits for them, and re-layouts  1.38 us (2%)
    pallas_call x1, Pallas kernels, on_device(): pl.pallas_call(kernel, out_shape=jax.ShapeDtypeStruct((64, 256), BF), in_...  78.8 us

profile of v2, /device:TPU:1, one launch (start us, length us, event | category | flops | bytes accessed | tf_op | source)
XLA Modules:
  0.0 80.8 jit_solution(167158954352944675)
XLA Ops:
  0.7 78.8 %shard_map.46 = bf16[64,256]{1,0:T(8,128)(2,1)} custom-call(bf16[256,512]{1,0:T(8,128)(2,1)} %tokens_hbm.1, bf16[3,64,256]{2,1,0:T(8,128)(2,1)} %bitcast.2, s32[1,128]{1,0:T(1,128)} %bitcast.3, s32[1]{0:T(128)S(6)} %copy.6.count_hbm), custom_call_target="tpu_custom_call" | custom-call | tf_op jit(solution)/shard_map/pallas_call | solution.py:323
  79.4 1.4 %copy.7 = bf16[64,256]{1,0:T(8,128)(2,1)} copy(bf16[64,256]{1,0:T(8,128)(2,1)} %shard_map.46) | data formatting | bytes 65536

commit v3 on v2

v3 whole, which is shorter than its diff:
```python
import heapq

import jax
import jax.numpy as jnp
from jax import lax
from jax.experimental import pallas as pl
from jax.experimental.pallas import tpu as pltpu
from jax.sharding import PartitionSpec as P

MESH = pl.DeviceIdType.MESH
NX, NY, NZ = 4, 8, 8
HD = 128
BF = jnp.bfloat16
F32 = jnp.float32
I32 = jnp.int32
GROUPS = 96
PHASES = 8
PEERS = sorted(
    ((dy, dx, dc) for dy in range(NY) for dx in range(NX) for dc in range(2) if dy or dx or dc),
    key=lambda p: -min(p[0], NY - p[0]) - min(p[1], NX - p[1]),
)


class Links:
    def __init__(self, send_sem, recv_sem):
        self.send_sem, self.recv_sem, self.phases, self.count = send_sem, recv_sem, 0, 0

    def group(self):
        self.count += 1
        return self.recv_sem.at[self.count - 1]

    def phase(self):
        self.phases += 1
        return self.send_sem.at[self.phases - 1]

    def send(self, src, dst, device, group, phase):
        pltpu.make_async_remote_copy(
            src_ref=src,
            dst_ref=dst,
            send_sem=phase,
            recv_sem=group,
            device_id=device,
            device_id_type=MESH,
        ).start()


def await_bytes(size, semaphore):
    pltpu.make_async_copy(size, size, semaphore).wait()


class Gather:
    ONE, ONE_A, ONE_B = (0, 48), (0, 32), (32, 48)
    TWO, TWO_A, TWO_B = (48, 128), (48, 96), (96, 128)

    def __init__(self, links, buf, place, unit, complete=None):
        self.links, self.buf, self.unit, self.complete = links, buf, unit, complete
        self.phase = links.phase()
        self.x, self.y, self.dev = place
        self.clock, self.busy, self.queue, self.number = 0.0, {}, [], 0
        self.missing = {0: 3, 1: 5, 2: 5, 3: 5, 4: 5}

    def col(self, k):
        return (self.x + k + NX) % NX

    def row(self, k):
        return (self.y + k + NY) % NY

    def send(self, group, row, col, rows, step):
        lo, hi = rows
        piece = self.buf.at[self.row(row) * NX + self.col(col), pl.ds(lo, hi - lo)]
        sy, sx = step
        to = self.dev(self.row(sy), self.col(sx))
        self.links.send(piece, piece, to, group[0], self.phase)
        self.clock += 0.06
        hops = abs(sy) + abs(sx)
        way = (sy > 0, sy < 0, sx > 0, sx < 0)
        end = max(self.busy.get(way, 0.0), self.clock) + (hi - lo) / 128 * self.unit * hops
        self.busy[way] = end
        group[1] = max(group[1], end + 1.95 + 0.65 * hops)
        group[2] += hi - lo

    def group(self):
        return [self.links.group(), 0.0, 0]

    def when(self, group, then):
        self.number += 1
        heapq.heappush(self.queue, (group[1], self.number, group, then))

    def advance(self, until):
        while self.queue and self.queue[0][0] <= until:
            at, _, (semaphore, _, rows), then = heapq.heappop(self.queue)
            blocks = 1 if rows <= 128 else rows // 80
            await_bytes(self.buf.at[pl.ds(0, blocks), pl.ds(0, rows // blocks)], semaphore)
            self.clock = max(self.clock, at)
            then()

    def finish(self):
        self.advance(1e9)

    def done(self, k):
        self.missing[k] -= 1
        if not self.missing[k] and self.complete:
            self.complete(k)

    def ring_y(self, cols, k=0):
        up = self.ONE_A if k == 3 else self.ONE
        down = self.ONE_B if k == 3 else self.ONE
        for col in cols:
            group = self.group()
            self.send(group, -k, col, up, (1, 0))
            self.send(group, k, col, down, (-1, 0))

            def arrived(col=col):
                if k < 3:
                    self.ring_y((col,), k + 1)
                self.done(k + 1)

            self.when(group, arrived)

    def tree_y(self):
        far, near = self.group(), self.group()
        self.send(far, 0, 0, self.TWO, (2, 0))
        self.send(far, 0, 0, self.TWO, (-2, 0))
        self.send(near, 0, 0, self.TWO, (1, 0))
        self.send(near, 0, 0, self.TWO, (-1, 0))

        def arrived():
            last, third = self.group(), self.group()
            self.send(last, -2, 0, self.TWO_A, (2, 0))
            self.send(last, 2, 0, self.TWO_B, (-2, 0))
            self.send(third, -2, 0, self.TWO, (1, 0))
            self.send(third, 2, 0, self.TWO, (-1, 0))
            self.when(third, lambda: self.ring_x((-3, 3)))
            self.when(last, lambda: self.ring_x((4,)))
            self.ring_x((-2, 2))

        self.when(near, lambda: self.ring_x((-1, 1)))
        self.when(far, arrived)

    def ring_x(self, rows):
        group = self.group()
        for r in rows:
            self.send(group, r, 0, self.TWO, (0, 1))
            self.send(group, r, 0, self.TWO, (0, -1))

        def arrived():
            rest = self.group()
            for r in rows:
                self.send(rest, r, -1, self.TWO_A, (0, 1))
                self.send(rest, r, 1, self.TWO_B, (0, -1))
            self.when(rest, lambda: self.done(abs(rows[0])))

        self.when(group, arrived)

    def start(self):
        group = self.group()
        self.send(group, 0, 0, self.ONE, (0, 1))
        self.send(group, 0, 0, self.ONE, (0, -1))

        def arrived():
            rest = self.group()
            self.send(rest, 0, -1, self.ONE_A, (0, 1))
            self.send(rest, 0, 1, self.ONE_B, (0, -1))

            def across():
                self.ring_y((2,))
                self.done(0)

            self.when(rest, across)
            self.ring_y((-1, 1))
            self.done(0)

        self.when(group, arrived)
        self.tree_y()
        self.ring_x((0,))
        self.ring_y((0,))


def iota(shape, axis):
    return lax.broadcasted_iota(I32, shape, axis)


def pick(mask, rows):
    ones = jnp.where(mask, 1.0, 0.0).astype(BF)
    return jnp.dot(ones, rows, preferred_element_type=F32).astype(BF)


def kernel(
    tokens_hbm, w, keep_hbm, count_hbm, out,
    tokens, keep, count, wbuf, kv, feats, cbuf, slots, outbox, inbox, heads, fin,
    send_sem, recv_sem, local_sem,
):
    s, z = lax.axis_index("seq"), lax.axis_index("tp")
    c = s % 2
    x = (s // 2) % NX
    y = s // (2 * NX)
    chip = s // 2

    def dev(yy, xx):
        return ((yy * NX + xx) * 2 + c, z)

    sibling = (s + 1 - 2 * c, z)
    peers = [(((y + p) % NY) * NX + (x + q) % NX) * 2 + (c + r) % 2 for p, q, r in PEERS]
    above = [(z + k) % NZ for k in range(NZ)]

    barrier = pltpu.get_barrier_semaphore()
    greet = [(p, z) for p in peers] + [(s, p) for p in above[1:]]
    for device in greet:
        pl.semaphore_signal(barrier, inc=1, device_id=device, device_id_type=MESH)

    mine, other = pl.multiple_of(c * HD, HD), pl.multiple_of((1 - c) * HD, HD)
    half = pl.ds(pl.multiple_of(c * 64, 64), 64)
    place = [wbuf.at[chip, half, pl.ds(g * HD, HD)] for g in range(3)]
    local = [
        pltpu.make_async_copy(count_hbm, count, local_sem.at[0]),
        pltpu.make_async_copy(keep_hbm, keep, local_sem.at[1]),
        pltpu.make_async_copy(tokens_hbm, tokens, local_sem.at[2]),
    ]
    for g in range(3):
        local.append(
            pltpu.make_async_copy(w.at[g, :, pl.ds(mine, HD)], place[g], local_sem.at[3 + g])
        )
    for copy in local:
        copy.start()
    for copy in local:
        copy.wait()
    cbuf[s] = jnp.full((1, 128), count[0], I32)
    chosen = (iota((256, 128), 0) == keep[...]).astype(F32).astype(BF)
    rows = lax.dot_general(
        chosen, tokens[...], (((0,), (0,)), ((), ())), preferred_element_type=F32
    ).astype(BF)
    for q in range(4):
        slots[q * 128 : (q + 1) * 128] = rows[:, q * 128 : (q + 1) * 128]
    pl.semaphore_wait(barrier, len(greet))

    links = Links(send_sem, recv_sem)
    rest = pl.ds(0, len(peers))
    swap_out, told_out, post_out, z_out, last_out = [links.phase() for _ in range(5)]

    swapped = links.group()
    for g in range(3):
        links.send(w.at[g, :, pl.ds(other, HD)], place[g], sibling, swapped, swap_out)
    told = links.group()
    for p in peers:
        links.send(cbuf.at[s], cbuf.at[s], (p, z), told, told_out)
    await_bytes(wbuf.at[0, pl.ds(0, 64)], swapped)
    weights = gather = Gather(links, wbuf, (x, y, dev), 1.97)
    gather.start()
    gather.advance(2.8)
    await_bytes(cbuf.at[rest], told)

    counts = cbuf[...].reshape(64, 128)
    shard = iota((64, 128), 0)
    begin = jnp.sum(jnp.where(shard < s, counts, 0), axis=0, keepdims=True)
    total = jnp.sum(jnp.where(shard == s, counts, 0), axis=0, keepdims=True)
    i = iota((1, 128), 1)
    code = jnp.where(i < total, ((begin + i) & 63) * 8 + (i >> 6), -8)
    code = jnp.concatenate([code + q * 2 for q in range(4)], axis=1)
    outbox[...] = pick(iota((512, 512), 0) == code, slots[...]).reshape(64, 8, 128)
    post = links.group()
    own = pltpu.make_async_copy(outbox.at[s], inbox.at[s], local_sem.at[6])
    own.start()
    for part in range(4):
        for p in peers[part * 16 : part * 16 + 16]:
            links.send(outbox.at[p], inbox.at[s], (p, z), post, post_out)
        gather.advance(4.8 + part)
    gather.advance(10.0)
    own.wait()
    wide = jnp.concatenate([counts] * 4, axis=1)
    shard, lane = iota((64, 512), 0), iota((64, 512), 1)
    begin = jnp.sum(jnp.where(shard < (lane >> 3), wide, 0), axis=0, keepdims=True)
    size = jnp.sum(jnp.where(shard == (lane >> 3), wide, 0), axis=0, keepdims=True)
    within = shard * 64 + s - begin
    live = (within >= 0) & (within < size) & ((within >> 6) == (lane & 1))
    block = (lane >> 1) & 3
    take = jnp.concatenate([live & (block == q) for q in range(4)], axis=0)
    await_bytes(inbox.at[rest], post)
    kept = pick(take, inbox[...].reshape(512, 128))
    feats[z * 2 + c] = jnp.concatenate([kept[q * 64 : (q + 1) * 64] for q in range(4)], axis=1)

    def over_z(group, k, lo, hi, step):
        piece = feats.at[above[k % NZ] * 2 + c, pl.ds(lo, hi - lo)]
        links.send(piece, piece, (s, above[step % NZ]), group, z_out)

    beside = {}

    def hand(*ks):
        group = links.group()
        for k in ks:
            piece = feats.at[above[k % NZ] * 2 + c]
            links.send(piece, piece, sibling, group, z_out)
        beside[ks] = group

    pair2, pair1, pair3, pair4 = [links.group() for _ in range(4)]
    two = feats.at[pl.ds(0, 2)]
    for k in (2, -2):
        over_z(pair2, 0, 0, 64, k)
    for k in (1, -1):
        over_z(pair1, 0, 0, 64, k)
    hand(0)
    gather.advance(17.0)
    await_bytes(two, pair2)
    over_z(pair4, -2, 0, 32, 2)
    over_z(pair4, 2, 32, 64, -2)
    over_z(pair3, -2, 0, 64, 1)
    over_z(pair3, 2, 0, 64, -1)
    hand(-2, 2)
    await_bytes(two, pair1)
    hand(-1, 1)
    gather.finish()

    acc = jnp.zeros((128, 384), F32)

    def project(acc, *ks):
        await_bytes(feats.at[pl.ds(0, len(ks))], beside[ks])
        for k in ks:
            zz = above[k % NZ]
            block = feats[pl.ds(zz * 2, 2)].reshape(128, 512)
            weight = wbuf[pl.ds(zz * NX, NX)].reshape(512, 384)
            acc = acc + jnp.dot(block, weight, preferred_element_type=F32)
        return acc

    acc = project(acc, 0)
    acc = project(acc, -2, 2)
    acc = project(acc, -1, 1)
    await_bytes(two, pair3)
    hand(-3, 3)
    await_bytes(feats.at[0], pair4)
    hand(4)
    acc = project(acc, -3, 3)
    acc = project(acc, 4)
    query = acc[:, :HD].astype(BF)
    kv[chip] = acc[:, HD:].astype(BF)

    qi, kj = iota((128, 512), 0), iota((128, 512), 1)
    lead = (kj & 63) * 64 + (kj >> 7) * 2 + ((kj >> 6) & 1)
    lead = lead - (qi & 63) * 64 - (qi >> 6) - chip * 2
    scale = HD ** (-0.5) * 1.4426950408889634
    state = [
        jnp.full((128, 1), -1e30, F32),
        jnp.zeros((128, 1), F32),
        jnp.zeros((128, HD), F32),
    ]

    def attend(k):
        for kk in sorted({-k, k}):
            if kk == -4:
                continue
            yy = (y + kk + NY) % NY
            top, denom, numer = state
            block = kv[pl.ds(yy * NX, NX)].reshape(512, 2 * HD)
            dots = lax.dot_general(
                query, block[:, :HD], (((1,), (1,)), ((), ())), preferred_element_type=F32
            ) * scale
            dots = jnp.where(lead > yy * -8, -jnp.inf, dots)
            high = jnp.maximum(top, jnp.max(dots, axis=1, keepdims=True))
            fade = jnp.exp2(top - high)
            expo = jnp.exp2(dots - high)
            state[0] = high
            state[1] = denom * fade + jnp.sum(expo, axis=1, keepdims=True)
            state[2] = numer * fade + jnp.dot(
                expo.astype(BF), block[:, HD:], preferred_element_type=F32
            )

    gather = Gather(links, kv, (x, y, dev), 1.31, attend)
    gather.start()
    gather.finish()
    heads[...] = (state[2] / state[1]).astype(BF).reshape(2, 64, HD)

    last = links.group()
    links.send(heads.at[1 - c], fin.at[c], sibling, last, last_out)
    own = pltpu.make_async_copy(heads.at[c], fin.at[c], local_sem.at[7])
    own.start()
    own.wait()
    await_bytes(fin.at[0], last)
    out[:, :HD] = fin[0]
    out[:, HD:] = fin[1]
    blocks = pl.ds(0, NX * NY - 1)
    sent = [
        (wbuf.at[0, pl.ds(0, 64)], swap_out),
        (cbuf.at[rest], told_out),
        (inbox.at[rest], post_out),
        (wbuf.at[blocks], weights.phase),
        (feats.at[pl.ds(0, 2 * NZ - 1)], z_out),
        (kv.at[blocks], gather.phase),
        (heads.at[0], last_out),
    ]
    for size, semaphore in sent:
        await_bytes(size, semaphore)


def on_device(tokens, w_qkv, keep_list, counts):
    hbm = pl.BlockSpec(memory_space=pltpu.HBM)
    return pl.pallas_call(
        kernel,
        out_shape=jax.ShapeDtypeStruct((64, 256), BF),
        in_specs=[hbm] * 4,
        out_specs=pl.BlockSpec(memory_space=pltpu.VMEM),
        scratch_shapes=[
            pltpu.VMEM((256, 512), BF),
            pltpu.VMEM((1, 128), I32),
            pltpu.SMEM((1,), I32),
            pltpu.VMEM((NY * NX, 128, 384), BF),
            pltpu.VMEM((NY * NX, 128, 256), BF),
            pltpu.VMEM((NZ * 2, 64, 512), BF),
            pltpu.VMEM((64, 1, 128), I32),
            pltpu.VMEM((512, 128), BF),
            pltpu.VMEM((64, 8, 128), BF),
            pltpu.VMEM((64, 8, 128), BF),
            pltpu.VMEM((2, 64, HD), BF),
            pltpu.VMEM((2, 64, HD), BF),
            pltpu.SemaphoreType.DMA((PHASES,)),
            pltpu.SemaphoreType.DMA((GROUPS,)),
            pltpu.SemaphoreType.DMA((8,)),
        ],
        compiler_params=pltpu.CompilerParams(
            collective_id=0, has_side_effects=True, vmem_limit_bytes=60 * 1024 * 1024
        ),
    )(tokens, jnp.transpose(w_qkv, (1, 0, 2)), keep_list.reshape(1, 128), counts)


def solution(mesh):
    in_specs = (P("seq", "tp"), P("seq", None, "tp"), P("seq"), P("seq"))
    return jax.shard_map(
        on_device, mesh=mesh, in_specs=in_specs, out_specs=P("seq", "tp"), check_vma=False
    )
```

time: 81 us -> 73.4 us (0.906)
  Pallas kernels: 78.8 us -> 71.1 us
    pallas_call x1, Pallas kernels: 78.8 us -> 71.1 us  [on_device(): pl.pallas_call(kernel, out_shape=jax.ShapeDtypeStruct((64, 256), BF), in_...]
where the time goes in v3:
time: 73.4 us; the launch traced here: 73.2 us
  Pallas kernels  71.1 us (97%)
  local copies, waits for them, and re-layouts  1.38 us (2%)
    pallas_call x1, Pallas kernels, on_device(): pl.pallas_call(kernel, out_shape=jax.ShapeDtypeStruct((64, 256), BF), in_...  71.1 us

profile of v3, /device:TPU:1, one launch (start us, length us, event | category | flops | bytes accessed | tf_op | source)
XLA Modules:
  0.0 73.2 jit_solution(16485326569898495576)
XLA Ops:
  0.7 71.1 %shard_map.46 = bf16[64,256]{1,0:T(8,128)(2,1)} custom-call(bf16[256,512]{1,0:T(8,128)(2,1)} %tokens_hbm.1, bf16[3,64,256]{2,1,0:T(8,128)(2,1)} %bitcast.2, s32[1,128]{1,0:T(1,128)} %bitcast.3, s32[1]{0:T(128)S(6)} %copy.6.count_hbm), custom_call_target="tpu_custom_call" | custom-call | tf_op jit(solution)/shard_map/pallas_call | solution.py:394
  71.8 1.4 %copy.7 = bf16[64,256]{1,0:T(8,128)(2,1)} copy(bf16[64,256]{1,0:T(8,128)(2,1)} %shard_map.46) | data formatting | bytes 65536

commit v4 on v3

--- a/solution.py
+++ b/solution.py
@@ -13,6 +13,7 @@
 BF = jnp.bfloat16
 F32 = jnp.float32
 I32 = jnp.int32
+T1, T2, T3 = 2.8, 9.0, 17.0
 GROUPS = 96
 PHASES = 8
 PEERS = sorted(
@@ -103,15 +104,18 @@
             self.complete(k)
 
     def ring_y(self, cols, k=0):
-        up = self.ONE_A if k == 3 else self.ONE
-        down = self.ONE_B if k == 3 else self.ONE
         for col in cols:
             group = self.group()
-            self.send(group, -k, col, up, (1, 0))
-            self.send(group, k, col, down, (-1, 0))
+            self.send(group, -k, col, self.ONE, (1, 0))
+            self.send(group, k, col, self.ONE, (-1, 0))
+            if k == 2:
+                last = self.group()
+                self.send(last, -2, col, self.ONE_A, (2, 0))
+                self.send(last, 2, col, self.ONE_B, (-2, 0))
+                self.when(last, lambda: self.done(4))
 
             def arrived(col=col):
-                if k < 3:
+                if k < 2:
                     self.ring_y((col,), k + 1)
                 self.done(k + 1)
 
@@ -222,31 +226,34 @@
         )
     for copy in local:
         copy.start()
-    for copy in local:
+    local[0].wait()
+    cbuf[s] = jnp.full((1, 128), count[0], I32)
+    pl.semaphore_wait(barrier, len(greet))
+
+    links = Links(send_sem, recv_sem)
+    rest = pl.ds(0, len(peers))
+    swap_out, told_out, post_out, z_out, last_out = [links.phase() for _ in range(5)]
+
+    swapped = links.group()
+    for g in range(3):
+        links.send(w.at[g, :, pl.ds(other, HD)], place[g], sibling, swapped, swap_out)
+    told = links.group()
+    for p in peers:
+        links.send(cbuf.at[s], cbuf.at[s], (p, z), told, told_out)
+    for copy in local[3:]:
         copy.wait()
-    cbuf[s] = jnp.full((1, 128), count[0], I32)
+    await_bytes(wbuf.at[0, pl.ds(0, 64)], swapped)
+    weights = gather = Gather(links, wbuf, (x, y, dev), 1.97)
+    gather.start()
+    for copy in local[1:3]:
+        copy.wait()
     chosen = (iota((256, 128), 0) == keep[...]).astype(F32).astype(BF)
     rows = lax.dot_general(
         chosen, tokens[...], (((0,), (0,)), ((), ())), preferred_element_type=F32
     ).astype(BF)
     for q in range(4):
         slots[q * 128 : (q + 1) * 128] = rows[:, q * 128 : (q + 1) * 128]
-    pl.semaphore_wait(barrier, len(greet))
-
-    links = Links(send_sem, recv_sem)
-    rest = pl.ds(0, len(peers))
-    swap_out, told_out, post_out, z_out, last_out = [links.phase() for _ in range(5)]
-
-    swapped = links.group()
-    for g in range(3):
-        links.send(w.at[g, :, pl.ds(other, HD)], place[g], sibling, swapped, swap_out)
-    told = links.group()
-    for p in peers:
-        links.send(cbuf.at[s], cbuf.at[s], (p, z), told, told_out)
-    await_bytes(wbuf.at[0, pl.ds(0, 64)], swapped)
-    weights = gather = Gather(links, wbuf, (x, y, dev), 1.97)
-    gather.start()
-    gather.advance(2.8)
+    gather.advance(T1)
     await_bytes(cbuf.at[rest], told)
 
     counts = cbuf[...].reshape(64, 128)
@@ -260,11 +267,9 @@
     post = links.group()
     own = pltpu.make_async_copy(outbox.at[s], inbox.at[s], local_sem.at[6])
     own.start()
-    for part in range(4):
-        for p in peers[part * 16 : part * 16 + 16]:
-            links.send(outbox.at[p], inbox.at[s], (p, z), post, post_out)
-        gather.advance(4.8 + part)
-    gather.advance(10.0)
+    for p in peers:
+        links.send(outbox.at[p], inbox.at[s], (p, z), post, post_out)
+    gather.advance(T2)
     own.wait()
     wide = jnp.concatenate([counts] * 4, axis=1)
     shard, lane = iota((64, 512), 0), iota((64, 512), 1)
@@ -298,7 +303,7 @@
     for k in (1, -1):
         over_z(pair1, 0, 0, 64, k)
     hand(0)
-    gather.advance(17.0)
+    gather.advance(T3)
     await_bytes(two, pair2)
     over_z(pair4, -2, 0, 32, 2)
     over_z(pair4, 2, 32, 64, -2)

time: 73.4 us -> 68.7 us (0.936)
  Pallas kernels: 71.1 us -> 66.5 us
    pallas_call x1, Pallas kernels: 71.1 us -> 66.5 us  [on_device(): pl.pallas_call(kernel, out_shape=jax.ShapeDtypeStruct((64, 256), BF), in_...]
where the time goes in v4:
time: 68.7 us; the launch traced here: 68.5 us
  Pallas kernels  66.5 us (97%)
  local copies, waits for them, and re-layouts  1.38 us (2%)
    pallas_call x1, Pallas kernels, on_device(): pl.pallas_call(kernel, out_shape=jax.ShapeDtypeStruct((64, 256), BF), in_...  66.5 us
    unnamed x1, local copies, waits for them, and re-layouts  1.38 us

profile of v4, /device:TPU:1, one launch (start us, length us, event | category | flops | bytes accessed | tf_op | source)
XLA Modules:
  0.0 68.5 jit_solution(438250473518386902)
XLA Ops:
  0.7 66.5 %shard_map.46 = bf16[64,256]{1,0:T(8,128)(2,1)} custom-call(bf16[256,512]{1,0:T(8,128)(2,1)} %tokens_hbm.1, bf16[3,64,256]{2,1,0:T(8,128)(2,1)} %bitcast.2, s32[1,128]{1,0:T(1,128)} %bitcast.3, s32[1]{0:T(128)S(6)} %copy.6.count_hbm), custom_call_target="tpu_custom_call" | custom-call | tf_op jit(solution)/shard_map/pallas_call | solution.py:399
  67.1 1.4 %copy.7 = bf16[64,256]{1,0:T(8,128)(2,1)} copy(bf16[64,256]{1,0:T(8,128)(2,1)} %shard_map.46) | data formatting | bytes 65536

commit v5 on v4

--- a/solution.py
+++ b/solution.py
@@ -13,9 +13,9 @@
 BF = jnp.bfloat16
 F32 = jnp.float32
 I32 = jnp.int32
-T1, T2, T3 = 2.8, 9.0, 17.0
-GROUPS = 96
-PHASES = 8
+T1, T2, T3, T4, T5 = 2.8, 9.0, 16.0, 20.0, 23.0
+GROUPS = 77
+PHASES = 7
 PEERS = sorted(
     ((dy, dx, dc) for dy in range(NY) for dx in range(NX) for dc in range(2) if dy or dx or dc),
     key=lambda p: -min(p[0], NY - p[0]) - min(p[1], NX - p[1]),
@@ -56,28 +56,28 @@
     def __init__(self, links, buf, place, unit, complete=None):
         self.links, self.buf, self.unit, self.complete = links, buf, unit, complete
         self.phase = links.phase()
-        self.x, self.y, self.dev = place
+        self.rows, self.cols, self.dev = place
         self.clock, self.busy, self.queue, self.number = 0.0, {}, [], 0
         self.missing = {0: 3, 1: 5, 2: 5, 3: 5, 4: 5}
 
     def col(self, k):
-        return (self.x + k + NX) % NX
+        return self.cols[k % NX]
 
     def row(self, k):
-        return (self.y + k + NY) % NY
+        return self.rows[k % NY]
 
     def send(self, group, row, col, rows, step):
         lo, hi = rows
         piece = self.buf.at[self.row(row) * NX + self.col(col), pl.ds(lo, hi - lo)]
         sy, sx = step
-        to = self.dev(self.row(sy), self.col(sx))
+        to = self.dev[sy % NY, sx % NX]
         self.links.send(piece, piece, to, group[0], self.phase)
         self.clock += 0.06
         hops = abs(sy) + abs(sx)
         way = (sy > 0, sy < 0, sx > 0, sx < 0)
         end = max(self.busy.get(way, 0.0), self.clock) + (hi - lo) / 128 * self.unit * hops
         self.busy[way] = end
-        group[1] = max(group[1], end + 1.95 + 0.65 * hops)
+        group[1] = max(group[1], end + 2.4 + 0.65 * hops)
         group[2] += hi - lo
 
     def group(self):
@@ -176,6 +176,9 @@
 
         self.when(group, arrived)
         self.tree_y()
+
+    def later(self, clock):
+        self.clock = max(self.clock, clock)
         self.ring_x((0,))
         self.ring_y((0,))
 
@@ -200,12 +203,16 @@
     y = s // (2 * NX)
     chip = s // 2
 
-    def dev(yy, xx):
-        return ((yy * NX + xx) * 2 + c, z)
-
+    rows = [lax.rem(y + k, NY) for k in range(NY)]
+    cols = [lax.rem(x + k, NX) for k in range(NX)]
+    dev = {
+        (p, q): ((rows[p] * NX + cols[q]) * 2 + c, z)
+        for p, q in ((0, 1), (0, 3), (1, 0), (7, 0), (2, 0), (6, 0))
+    }
+    plane = (rows, cols, dev)
     sibling = (s + 1 - 2 * c, z)
-    peers = [(((y + p) % NY) * NX + (x + q) % NX) * 2 + (c + r) % 2 for p, q, r in PEERS]
-    above = [(z + k) % NZ for k in range(NZ)]
+    peers = [(rows[p] * NX + cols[q]) * 2 + (1 - c if r else c) for p, q, r in PEERS]
+    above = [lax.rem(z + k, NZ) for k in range(NZ)]
 
     barrier = pltpu.get_barrier_semaphore()
     greet = [(p, z) for p in peers] + [(s, p) for p in above[1:]]
@@ -243,18 +250,34 @@
     for copy in local[3:]:
         copy.wait()
     await_bytes(wbuf.at[0, pl.ds(0, 64)], swapped)
-    weights = gather = Gather(links, wbuf, (x, y, dev), 1.97)
+    waiting, features = [], []
+    projected = [jnp.zeros((128, 384), F32)]
+
+    def project(k):
+        for kk in sorted({-k % NY, k}):
+            block = feats[pl.ds(rows[kk] * 2, 2)].reshape(128, 512)
+            weight = wbuf[pl.ds(rows[kk] * NX, NX)].reshape(512, 384)
+            projected[0] = projected[0] + jnp.dot(block, weight, preferred_element_type=F32)
+
+    def here(k):
+        if features:
+            project(k)
+        else:
+            waiting.append(k)
+
+    weights = gather = Gather(links, wbuf, plane, 1.97, here)
     gather.start()
     for copy in local[1:3]:
         copy.wait()
     chosen = (iota((256, 128), 0) == keep[...]).astype(F32).astype(BF)
-    rows = lax.dot_general(
+    picked = lax.dot_general(
         chosen, tokens[...], (((0,), (0,)), ((), ())), preferred_element_type=F32
     ).astype(BF)
     for q in range(4):
-        slots[q * 128 : (q + 1) * 128] = rows[:, q * 128 : (q + 1) * 128]
+        slots[q * 128 : (q + 1) * 128] = picked[:, q * 128 : (q + 1) * 128]
     gather.advance(T1)
     await_bytes(cbuf.at[rest], told)
+    gather.later(3.0)
 
     counts = cbuf[...].reshape(64, 128)
     shard = iota((64, 128), 0)
@@ -269,8 +292,6 @@
     own.start()
     for p in peers:
         links.send(outbox.at[p], inbox.at[s], (p, z), post, post_out)
-    gather.advance(T2)
-    own.wait()
     wide = jnp.concatenate([counts] * 4, axis=1)
     shard, lane = iota((64, 512), 0), iota((64, 512), 1)
     begin = jnp.sum(jnp.where(shard < (lane >> 3), wide, 0), axis=0, keepdims=True)
@@ -279,6 +300,8 @@
     live = (within >= 0) & (within < size) & ((within >> 6) == (lane & 1))
     block = (lane >> 1) & 3
     take = jnp.concatenate([live & (block == q) for q in range(4)], axis=0)
+    gather.advance(T2)
+    own.wait()
     await_bytes(inbox.at[rest], post)
     kept = pick(take, inbox[...].reshape(512, 128))
     feats[z * 2 + c] = jnp.concatenate([kept[q * 64 : (q + 1) * 64] for q in range(4)], axis=1)
@@ -312,28 +335,19 @@
     hand(-2, 2)
     await_bytes(two, pair1)
     hand(-1, 1)
-    gather.finish()
-
-    acc = jnp.zeros((128, 384), F32)
-
-    def project(acc, *ks):
-        await_bytes(feats.at[pl.ds(0, len(ks))], beside[ks])
-        for k in ks:
-            zz = above[k % NZ]
-            block = feats[pl.ds(zz * 2, 2)].reshape(128, 512)
-            weight = wbuf[pl.ds(zz * NX, NX)].reshape(512, 384)
-            acc = acc + jnp.dot(block, weight, preferred_element_type=F32)
-        return acc
-
-    acc = project(acc, 0)
-    acc = project(acc, -2, 2)
-    acc = project(acc, -1, 1)
+    gather.advance(T4)
     await_bytes(two, pair3)
     hand(-3, 3)
     await_bytes(feats.at[0], pair4)
     hand(4)
-    acc = project(acc, -3, 3)
-    acc = project(acc, 4)
+    gather.advance(T5)
+    for ks, group in beside.items():
+        await_bytes(feats.at[pl.ds(0, len(ks))], group)
+    features.append(feats)
+    for k in waiting:
+        project(k)
+    gather.finish()
+    acc = projected[0]
     query = acc[:, :HD].astype(BF)
     kv[chip] = acc[:, HD:].astype(BF)
 
@@ -348,10 +362,8 @@
     ]
 
     def attend(k):
-        for kk in sorted({-k, k}):
-            if kk == -4:
-                continue
-            yy = (y + kk + NY) % NY
+        for kk in sorted({-k % NY, k}):
+            yy = rows[kk]
             top, denom, numer = state
             block = kv[pl.ds(yy * NX, NX)].reshape(512, 2 * HD)
             dots = lax.dot_general(
@@ -367,8 +379,9 @@
                 expo.astype(BF), block[:, HD:], preferred_element_type=F32
             )
 
-    gather = Gather(links, kv, (x, y, dev), 1.31, attend)
+    gather = Gather(links, kv, plane, 1.31, attend)
     gather.start()
+    gather.later(0.0)
     gather.finish()
     heads[...] = (state[2] / state[1]).astype(BF).reshape(2, 64, HD)
 

time: 68.7 us -> 67.1 us (0.977)
  Pallas kernels: 66.5 us -> 64.9 us
    pallas_call x1, Pallas kernels: 66.5 us -> 64.9 us  [on_device(): pl.pallas_call(kernel, out_shape=jax.ShapeDtypeStruct((64, 256), BF), in_...]
where the time goes in v5:
time: 67.1 us; the launch traced here: 66.9 us
  Pallas kernels  64.9 us (97%)
  local copies, waits for them, and re-layouts  1.38 us (2%)
    pallas_call x1, Pallas kernels, on_device(): pl.pallas_call(kernel, out_shape=jax.ShapeDtypeStruct((64, 256), BF), in_...  64.9 us
    unnamed x1, local copies, waits for them, and re-layouts  1.38 us

profile of v5, /device:TPU:1, one launch (start us, length us, event | category | flops | bytes accessed | tf_op | source)
XLA Modules:
  0.0 66.9 jit_solution(11349039885843263823)
XLA Ops:
  0.7 64.9 %shard_map.46 = bf16[64,256]{1,0:T(8,128)(2,1)} custom-call(bf16[256,512]{1,0:T(8,128)(2,1)} %tokens_hbm.1, bf16[3,64,256]{2,1,0:T(8,128)(2,1)} %bitcast.2, s32[1,128]{1,0:T(1,128)} %bitcast.3, s32[1]{0:T(128)S(6)} %copy.6.count_hbm), custom_call_target="tpu_custom_call" | custom-call | tf_op jit(solution)/shard_map/pallas_call | solution.py:412
  65.5 1.4 %copy.7 = bf16[64,256]{1,0:T(8,128)(2,1)} copy(bf16[64,256]{1,0:T(8,128)(2,1)} %shard_map.46) | data formatting | bytes 65536

commit v6 on v5

--- a/solution.py
+++ b/solution.py
@@ -77,7 +77,7 @@
         way = (sy > 0, sy < 0, sx > 0, sx < 0)
         end = max(self.busy.get(way, 0.0), self.clock) + (hi - lo) / 128 * self.unit * hops
         self.busy[way] = end
-        group[1] = max(group[1], end + 2.4 + 0.65 * hops)
+        group[1] = max(group[1], end + (2.8 if self.unit > 1.5 else 2.0) + 0.65 * hops)
         group[2] += hi - lo
 
     def group(self):

time: 67.1 us -> 67 us (level)
  no operation moved by 1% of the time
where the time goes in v6:
time: 67 us; the launch traced here: 66.8 us
  Pallas kernels  64.8 us (97%)
  local copies, waits for them, and re-layouts  1.38 us (2%)
    pallas_call x1, Pallas kernels, on_device(): pl.pallas_call(kernel, out_shape=jax.ShapeDtypeStruct((64, 256), BF), in_...  64.8 us
    unnamed x1, local copies, waits for them, and re-layouts  1.38 us

profile of v6, /device:TPU:1, one launch (start us, length us, event | category | flops | bytes accessed | tf_op | source)
XLA Modules:
  0.0 66.8 jit_solution(9994203576608193046)
XLA Ops:
  0.7 64.8 %shard_map.46 = bf16[64,256]{1,0:T(8,128)(2,1)} custom-call(bf16[256,512]{1,0:T(8,128)(2,1)} %tokens_hbm.1, bf16[3,64,256]{2,1,0:T(8,128)(2,1)} %bitcast.2, s32[1,128]{1,0:T(1,128)} %bitcast.3, s32[1]{0:T(128)S(6)} %copy.6.count_hbm), custom_call_target="tpu_custom_call" | custom-call | tf_op jit(solution)/shard_map/pallas_call | solution.py:412
  65.5 1.4 %copy.7 = bf16[64,256]{1,0:T(8,128)(2,1)} copy(bf16[64,256]{1,0:T(8,128)(2,1)} %shard_map.46) | data formatting | bytes 65536
